TPU v7x, 32 devices: a whole 2x2x4 slice. The times are simulated.
32 devices in a mesh: panel: 8 (over z, x), obs: 4 (over y, core).
Axes of the slice: x: 2, y: 2, z: 4, core: 2. Of those that a mesh axis runs over, the one named last changes fastest.
Arguments:
- samples: bfloat16 [1024, 4, 4096], P(('panel', 'obs')), may hold values from -6 to 6
- panel_position: float32 [3, 4096], P(None, 'panel'), may hold values from -1 to 1
- panel_area: float32 [4096], P('panel'), may hold values from 0.5 to 2
- panel_counts: int32 [32], P('panel'), may hold values from 1 to 128
- obs_position: float32 [3, 1024], P(None, 'obs'), may hold values from -12 to 12, as said below
- freq_bins: int32 [32], replicated, may hold values from 1 to 511
Outputs:
- far_pressure: float32 [2, 32, 1024], P(None, None, ('obs', 'panel'))
Inputs may be any that keep to these rules, and one draw needn't show every extreme that they name: `obs_position`: observers lie at distances 6 to 12 from the anchor.
All inputs are finite; a program needn't handle non-finite values.
Results may differ from a plain program's by a relative error of at most 0.0027.
Values may be sent and summed in bfloat16 or wider, within the bound.
A program may use at most 64 MiB of HBM per device.

v0:
```python
import math

import jax
import jax.numpy as jnp
from jax import lax
from jax.sharding import PartitionSpec as P

TIME = 1024
NF = 32
FBLK = 4


SPACING = 0.1


def make_table(time_rows, freq_bins):
    phase_index = freq_bins[None, :] * time_rows[:, None] % TIME
    angle_arg = 2.0 * math.pi / TIME * phase_index.astype(jnp.float32)
    window = 0.5 - 0.5 * jnp.cos(2.0 * math.pi / TIME * time_rows.astype(jnp.float32))
    weight = 2.0 / TIME * window[:, None]
    return jnp.concatenate(
        [weight * jnp.cos(angle_arg), -weight * jnp.sin(angle_arg)], axis=1
    ).astype(jnp.bfloat16)


def live_rows(counts):
    lane_ids = jnp.arange(128, dtype=jnp.int32)
    return (lane_ids[None, :] < counts[:, None]).astype(jnp.float32).reshape(-1)


def transform(window_table, turned):
    flat_samples = turned.reshape(window_table.shape[0], -1)
    raw_spectra = lax.dot_general(
        window_table, flat_samples, (((0,), (0,)), ((), ())), preferred_element_type=jnp.float32
    )
    return raw_spectra.reshape(2 * NF, 4, -1)


def radiate(obs_position, panel_position, panel_area, spectra, freq_bins):
    offset = obs_position[:, :, None] - panel_position[:, None, :]
    distance = jnp.sqrt(jnp.sum(offset * offset, axis=0))
    inverse = 1.0 / distance
    unit_dir = offset * inverse[None]
    green_scale = panel_area[None, :] * inverse * (1.0 / (4.0 * math.pi))
    freq_count = freq_bins.shape[0]
    real_blocks = spectra[:freq_count].reshape(freq_count // FBLK, FBLK, 4, -1)
    imag_blocks = spectra[freq_count:].reshape(freq_count // FBLK, FBLK, 4, -1)
    bin_blocks = freq_bins.reshape(freq_count // FBLK, FBLK)

    def one_block(block_items):
        real_src, imag_src, bin_block = block_items
        wavenumber = (2.0 * math.pi / (TIME * SPACING) * bin_block.astype(jnp.float32))[
            :, None, None
        ]
        radial_real = jnp.sum(unit_dir[None] * real_src[:, 1:, None, :], axis=1)
        radial_imag = jnp.sum(unit_dir[None] * imag_src[:, 1:, None, :], axis=1)
        source_real = (
            -wavenumber * imag_src[:, 0][:, None, :]
            + radial_real * inverse[None]
            - wavenumber * radial_imag
        )
        source_imag = (
            wavenumber * real_src[:, 0][:, None, :]
            + wavenumber * radial_real
            + radial_imag * inverse[None]
        )
        phase_arg = wavenumber * distance[None]
        cosine = jnp.cos(phase_arg)
        sine_part = jnp.sin(phase_arg)
        out_real = jnp.sum(
            green_scale[None] * (cosine * source_real + sine_part * source_imag), axis=2
        )
        out_imag = jnp.sum(
            green_scale[None] * (cosine * source_imag - sine_part * source_real), axis=2
        )
        return jnp.stack([out_real, out_imag])

    result = lax.map(one_block, (real_blocks, imag_blocks, bin_blocks))
    return jnp.transpose(result, (1, 0, 2, 3)).reshape(2, freq_count, -1)


def shards(samples, panel_position, panel_area, panel_counts, obs_position, freq_bins):
    slab_len = samples.shape[0]
    panel_count = lax.axis_size("panel")
    obs_count = lax.axis_size("obs")
    source_slabs = jnp.arange(panel_count, dtype=jnp.int32)
    inner_step = jnp.arange(slab_len, dtype=jnp.int32)
    turned = lax.all_to_all(
        lax.all_to_all(samples, "panel", split_axis=2, concat_axis=0, tiled=True),
        "obs",
        split_axis=2,
        concat_axis=0,
        tiled=True,
    )
    quarters = jnp.arange(obs_count, dtype=jnp.int32)
    time_rows = (
        (source_slabs[None, :, None] * obs_count + quarters[:, None, None]) * slab_len
        + inner_step[None, None, :]
    ).reshape(-1)
    local_spectra = transform(make_table(time_rows, freq_bins), turned)
    spectra = lax.all_gather(local_spectra, "obs", axis=2, tiled=True)
    sources = spectra * live_rows(panel_counts)[None, None, :]
    partial_field = radiate(obs_position, panel_position, panel_area, sources, freq_bins)
    return lax.psum_scatter(partial_field, "panel", scatter_dimension=2, tiled=True)


def solution(mesh):
    in_specs = (
        P(("panel", "obs"), None, None),
        P(None, "panel"),
        P("panel"),
        P("panel"),
        P(None, "obs"),
        P(),
    )
    out_specs = P(None, None, ("obs", "panel"))
    return jax.shard_map(shards, mesh=mesh, in_specs=in_specs, out_specs=out_specs, check_vma=False)
```

profile of v0, /device:TPU:0, one launch (start us, length us, event | category | flops | bytes accessed | tf_op | source)
XLA Modules:
  0.0 253.2 jit_solution(14489346298555074122)
XLA Ops:
  6.5 7.2 %copy.44 = bf16[32,4,4096]{0,1,2:T(4,128)(2,1)} copy(bf16[32,4,4096]{2,1,0:T(4,128)(2,1)} %param.8) | data formatting | bytes 2097152 | tf_op args[0]
  13.7 7.8 %reshape.142 = bf16[8,2,32768]{2,1,0:T(2,128)(2,1)} reshape(bf16[4096,4,32]{2,1,0:T(4,128)(2,1)} %bitcast.66) | data formatting | bytes 2097152
  21.6 7.4 %all-to-all-start = ((bf16[8,2,32768]{2,1,0:T(2,128)(2,1)}), bf16[8,2,32768]{2,1,0:T(2,128)(2,1)S(1)}, u32[]{:S(2)}, u32[]{:S(2)}) async-start(bf16[8,2,32768]{2,1,0:T(2,128)(2,1)} %reshape.142), calls=%async_computation | async-start | bytes 2097152 | tf_op jit(solution)/shard_map/all_to_all | solution.py:89
  29.1 25.6 %all-to-all-done = bf16[8,2,32768]{2,1,0:T(2,128)(2,1)S(1)} async-done(((bf16[8,2,32768]{2,1,0:T(2,128)(2,1)}), bf16[8,2,32768]{2,1,0:T(2,128)(2,1)S(1)}, u32[]{:S(2)}, u32[]{:S(2)}) %all-to-all-start) | async-done | bytes 1048608 | tf_op jit(solution)/shard_map/all_to_all | solution.py:89
  54.7 4.5 %reshape.143 = bf16[4096,4,32]{2,1,0:T(4,128)(2,1)} reshape(bf16[8,2,32768]{2,1,0:T(2,128)(2,1)S(1)} %all-to-all-done) | data formatting | bytes 2097152
  59.2 5.5 %copy.55 = bf16[32,4,8,512]{3,0,2,1:T(8,128)(2,1)S(1)} copy(bf16[32,4,8,512]{0,1,3,2:T(4,128)(2,1)} %bitcast.65) | data formatting | bytes 2097152 | tf_op jit(solution)/shard_map/all_to_all | solution.py:89
  64.8 1.4 copy.47
  66.2 3.5 %all-to-all-start.1 = ((bf16[256,4,512]{0,1,2:T(4,128)(2,1)}), bf16[256,4,512]{0,1,2:T(4,128)(2,1)S(1)}, u32[]{:S(2)}, u32[]{:S(2)}) async-start(bf16[256,4,512]{0,1,2:T(4,128)(2,1)} %copy.47), calls=%async_computation.1 | async-start | bytes 2097152 | tf_op jit(solution)/shard_map/all_to_all | solution.py:88
  69.8 1.0 multiply_reduce_fusion.2
  70.8 0.1 reshape.133
  71.0 0.6 multiply_convert_fusion.1
  71.6 1.3 fusion.28
  73.0 11.2 %all-to-all-done.1 = bf16[256,4,512]{0,1,2:T(4,128)(2,1)S(1)} async-done(((bf16[256,4,512]{0,1,2:T(4,128)(2,1)}), bf16[256,4,512]{0,1,2:T(4,128)(2,1)S(1)}, u32[]{:S(2)}, u32[]{:S(2)}) %all-to-all-start.1) | async-done | bytes 1048608 | tf_op jit(solution)/shard_map/all_to_all | solution.py:88
  84.1 1.1 copy.48
  85.3 1.6 copy.49
  86.9 1.2 copy.62
  88.0 1.5 copy.50
  89.5 0.4 fusion.21
  90.0 6.6 %all_gather.3 = f32[64,4,512]{2,0,1:T(8,128)S(1)} all-gather(f32[64,4,128]{2,0,1:T(8,128)S(1)} %fusion.21), channel_id=1, replica_groups=mesh['panel'=8,'obs'=4] {'obs'}, dimensions={2}, use_global_device_ids=true | all-gather | bytes 655360 | tf_op jit(solution)/shard_map/all_gather | solution.py:101
  96.7 0.1 reshape.136
  96.7 0.1 reshape.135
  96.8 87.3 %while.11 = (s32[]{:T(128)}, f32[8,2,4,256]{3,2,1,0:T(4,128)S(1)}, f32[256,512]{1,0:T(8,128)S(1)}, s32[8,4]{1,0:T(8,128)S(1)}, f32[256,512]{1,0:T(8,128)S(1)}, /...) while((s32[]{:T(128)}, f32[8,2,4,256]{3,2,1,0:T(4,128)S(1)}, ...), condition=%wide.region_6.7_spmd.clone, body=%wide.region_1.6_spmd.clone.sunk | while | flops 15994894 | bytes 14091497 | solution.py:78
  96.9 0.1 fusion.37
  97.0 0.1 fusion.38
  97.1 0.2 subtract_multiply_fusion.3
  97.3 1.0 multiply_reduce_fusion.4
  98.3 9.4 %fusion.39 = (f32[4,256]{1,0:T(4,128)S(1)}, f32[4,256]{1,0:T(4,128)S(1)}) fusion(f32[256,512]{1,0:T(8,128)S(1)} %get-tuple-element.297, f32[4]{0:T(128)S(1)} %get-tuple-element.261, f32[256,512]{1,0:T(8,128)S(1)} %get-tuple-element.295, f32[4,256,512]{2,1,0:T(8,128)S(1)} %get-tuple-element.264, f32[4,256,512]{2,1,0:T(8,128)S(1)} %get-tuple-element.265, ...), kind=kLoop, calls=%fused_computation.11.clone.1 | loop fusion | flops 9959424 | bytes 5791760 | tf_op jit(solution)/shard_map/while/body/eval_jaxpr/reduce_sum | solution.py:70
  107.8 0.1 fusion.37
  107.9 0.1 fusion.38
  108.0 0.2 subtract_multiply_fusion.3
  108.2 1.0 multiply_reduce_fusion.4
  109.2 9.4 %fusion.39 = (f32[4,256]{1,0:T(4,128)S(1)}, f32[4,256]{1,0:T(4,128)S(1)}) fusion(f32[256,512]{1,0:T(8,128)S(1)} %get-tuple-element.297, f32[4]{0:T(128)S(1)} %get-tuple-element.261, f32[256,512]{1,0:T(8,128)S(1)} %get-tuple-element.295, f32[4,256,512]{2,1,0:T(8,128)S(1)} %get-tuple-element.264, f32[4,256,512]{2,1,0:T(8,128)S(1)} %get-tuple-element.265, ...), kind=kLoop, calls=%fused_computation.11.clone.1 | loop fusion | flops 9959424 | bytes 5791760 | tf_op jit(solution)/shard_map/while/body/eval_jaxpr/reduce_sum | solution.py:70
  118.7 0.1 fusion.37
  118.8 0.1 fusion.38
  118.9 0.2 subtract_multiply_fusion.3
  119.1 1.0 multiply_reduce_fusion.4
  120.1 9.4 %fusion.39 = (f32[4,256]{1,0:T(4,128)S(1)}, f32[4,256]{1,0:T(4,128)S(1)}) fusion(f32[256,512]{1,0:T(8,128)S(1)} %get-tuple-element.297, f32[4]{0:T(128)S(1)} %get-tuple-element.261, f32[256,512]{1,0:T(8,128)S(1)} %get-tuple-element.295, f32[4,256,512]{2,1,0:T(8,128)S(1)} %get-tuple-element.264, f32[4,256,512]{2,1,0:T(8,128)S(1)} %get-tuple-element.265, ...), kind=kLoop, calls=%fused_computation.11.clone.1 | loop fusion | flops 9959424 | bytes 5791760 | tf_op jit(solution)/shard_map/while/body/eval_jaxpr/reduce_sum | solution.py:70
  129.7 0.1 fusion.38
  129.8 0.2 subtract_multiply_fusion.3
  130.0 1.0 multiply_reduce_fusion.4
  131.0 9.4 %fusion.39 = (f32[4,256]{1,0:T(4,128)S(1)}, f32[4,256]{1,0:T(4,128)S(1)}) fusion(f32[256,512]{1,0:T(8,128)S(1)} %get-tuple-element.297, f32[4]{0:T(128)S(1)} %get-tuple-element.261, f32[256,512]{1,0:T(8,128)S(1)} %get-tuple-element.295, f32[4,256,512]{2,1,0:T(8,128)S(1)} %get-tuple-element.264, f32[4,256,512]{2,1,0:T(8,128)S(1)} %get-tuple-element.265, ...), kind=kLoop, calls=%fused_computation.11.clone.1 | loop fusion | flops 9959424 | bytes 5791760 | tf_op jit(solution)/shard_map/while/body/eval_jaxpr/reduce_sum | solution.py:70
  140.5 0.1 fusion.37
  140.6 0.1 fusion.38
  140.7 0.2 subtract_multiply_fusion.3
  140.9 1.0 multiply_reduce_fusion.4
  141.9 9.4 %fusion.39 = (f32[4,256]{1,0:T(4,128)S(1)}, f32[4,256]{1,0:T(4,128)S(1)}) fusion(f32[256,512]{1,0:T(8,128)S(1)} %get-tuple-element.297, f32[4]{0:T(128)S(1)} %get-tuple-element.261, f32[256,512]{1,0:T(8,128)S(1)} %get-tuple-element.295, f32[4,256,512]{2,1,0:T(8,128)S(1)} %get-tuple-element.264, f32[4,256,512]{2,1,0:T(8,128)S(1)} %get-tuple-element.265, ...), kind=kLoop, calls=%fused_computation.11.clone.1 | loop fusion | flops 9959424 | bytes 5791760 | tf_op jit(solution)/shard_map/while/body/eval_jaxpr/reduce_sum | solution.py:70
  151.5 0.1 fusion.38
  151.6 0.2 subtract_multiply_fusion.3
  151.8 1.0 multiply_reduce_fusion.4
  152.8 9.4 %fusion.39 = (f32[4,256]{1,0:T(4,128)S(1)}, f32[4,256]{1,0:T(4,128)S(1)}) fusion(f32[256,512]{1,0:T(8,128)S(1)} %get-tuple-element.297, f32[4]{0:T(128)S(1)} %get-tuple-element.261, f32[256,512]{1,0:T(8,128)S(1)} %get-tuple-element.295, f32[4,256,512]{2,1,0:T(8,128)S(1)} %get-tuple-element.264, f32[4,256,512]{2,1,0:T(8,128)S(1)} %get-tuple-element.265, ...), kind=kLoop, calls=%fused_computation.11.clone.1 | loop fusion | flops 9959424 | bytes 5791760 | tf_op jit(solution)/shard_map/while/body/eval_jaxpr/reduce_sum | solution.py:70
  162.4 0.1 fusion.38
  162.5 0.2 subtract_multiply_fusion.3
  162.7 1.0 multiply_reduce_fusion.4
  163.8 9.4 %fusion.39 = (f32[4,256]{1,0:T(4,128)S(1)}, f32[4,256]{1,0:T(4,128)S(1)}) fusion(f32[256,512]{1,0:T(8,128)S(1)} %get-tuple-element.297, f32[4]{0:T(128)S(1)} %get-tuple-element.261, f32[256,512]{1,0:T(8,128)S(1)} %get-tuple-element.295, f32[4,256,512]{2,1,0:T(8,128)S(1)} %get-tuple-element.264, f32[4,256,512]{2,1,0:T(8,128)S(1)} %get-tuple-element.265, ...), kind=kLoop, calls=%fused_computation.11.clone.1 | loop fusion | flops 9959424 | bytes 5791760 | tf_op jit(solution)/shard_map/while/body/eval_jaxpr/reduce_sum | solution.py:70
  173.2 0.1 fusion.37
  173.3 0.1 fusion.38
  173.4 0.2 subtract_multiply_fusion.3
  173.6 1.0 multiply_reduce_fusion.4
  174.7 9.4 %fusion.39 = (f32[4,256]{1,0:T(4,128)S(1)}, f32[4,256]{1,0:T(4,128)S(1)}) fusion(f32[256,512]{1,0:T(8,128)S(1)} %get-tuple-element.297, f32[4]{0:T(128)S(1)} %get-tuple-element.261, f32[256,512]{1,0:T(8,128)S(1)} %get-tuple-element.295, f32[4,256,512]{2,1,0:T(8,128)S(1)} %get-tuple-element.264, f32[4,256,512]{2,1,0:T(8,128)S(1)} %get-tuple-element.265, ...), kind=kLoop, calls=%fused_computation.11.clone.1 | loop fusion | flops 9959424 | bytes 5791760 | tf_op jit(solution)/shard_map/while/body/eval_jaxpr/reduce_sum | solution.py:70
  184.2 0.1 copy.56
  184.3 0.8 reshape.140
  185.2 59.7 %reduce-scatter.4.cloned.1.call-done = f32[32,64]{1,0:T(8,128)} async-done(((f32[256,64]{1,0:T(8,128)}), f32[32,64]{1,0:T(8,128)}) %reduce-scatter.4.cloned.1.call-update) | async-done | bytes 8208
  244.9 0.8 reshape.141
  245.7 0.7 copy.57
  (82 shorter events, 1.3 us)
Async XLA Ops:
  21.6 7.4 %copy-start.4 = (s32[4]{0:T(128)S(1)}, s32[4]{0:T(128)}, u32[]{:S(2)}) copy-start(s32[4]{0:T(128)} %param.11) | copy-start | bytes 52
  21.6 33.2 %all-to-all-start = ((bf16[8,2,32768]{2,1,0:T(2,128)(2,1)}), bf16[8,2,32768]{2,1,0:T(2,128)(2,1)S(1)}, u32[]{:S(2)}, u32[]{:S(2)}) async-start(bf16[8,2,32768]{2,1,0:T(2,128)(2,1)} %reshape.142), calls=%async_computation | async-start | bytes 2097152 | tf_op jit(solution)/shard_map/all_to_all | solution.py:89
  64.7 5.0 %copy-start = (f32[3,512]{1,0:T(4,128)S(1)}, f32[3,512]{1,0:T(4,128)}, u32[]{:S(2)}) copy-start(f32[3,512]{1,0:T(4,128)} %param.9) | copy-start | bytes 18436
  64.7 5.0 %copy-start.1 = (f32[3,256]{1,0:T(4,128)S(1)}, f32[3,256]{1,0:T(4,128)}, u32[]{:S(2)}) copy-start(f32[3,256]{1,0:T(4,128)} %param.12) | copy-start | bytes 9220
  64.8 6.1 %copy-start.2 = (s32[32]{0:T(128)S(1)}, s32[32]{0:T(128)}, u32[]{:S(2)}) copy-start(s32[32]{0:T(128)} %param.13) | copy-start | bytes 388
  64.8 6.9 %copy-start.3 = (f32[512]{0:T(512)S(1)}, f32[512]{0:T(512)}, u32[]{:S(2)}) copy-start(f32[512]{0:T(512)} %param.10) | copy-start | bytes 6148
  66.2 18.0 %all-to-all-start.1 = ((bf16[256,4,512]{0,1,2:T(4,128)(2,1)}), bf16[256,4,512]{0,1,2:T(4,128)(2,1)S(1)}, u32[]{:S(2)}, u32[]{:S(2)}) async-start(bf16[256,4,512]{0,1,2:T(4,128)(2,1)} %copy.47), calls=%async_computation.1 | async-start | bytes 2097152 | tf_op jit(solution)/shard_map/all_to_all | solution.py:88
  69.7 175.2 %reduce-scatter.4.cloned.1.call-start = ((), (), s32[]{:S(2)}) async-start(), calls=%async_computation.3 | async-start | bytes 147456
Sparse Core Ops, SparseCore 0:
  185.3 59.5 reduce-scatter.3
where the time goes:
time: 254 us; the launch traced here: 253 us
  waiting for transfers between devices  96.5 us (38%)
  other arithmetic  89.6 us (35%)
  local copies, waits for them, and re-layouts  35.1 us (14%)
  between operations  13.6 us (5%)
  starting transfers between devices  10.9 us (4%)
  blocking collectives  6.58 us (3%)
    reduce_sum x8, other arithmetic, one_block(): jnp.sum(green_scale[None] * (cosine * source_real + sine_part * source_im...  75.3 us
    unnamed x2, waiting for transfers between devices  59.7 us
    all_to_all x1, waiting for transfers between devices, shards(): lax.all_to_all(samples, 'panel', split_axis=2, concat_axis=0, tiled=True)  25.6 us
    unnamed x18, local copies, waits for them, and re-layouts  23.2 us
    all_to_all x1, waiting for transfers between devices, shards(): lax.all_to_all(lax.all_to_all(samples, 'panel', split_axis=2, concat_axis...  11.2 us
    reduce_sum x8, other arithmetic, one_block(): radial_real = jnp.sum(unit_dir[None] * real_src[:, 1:, None, :], axis=1)  8.15 us
    all_to_all x1, starting transfers between devices, shards(): lax.all_to_all(samples, 'panel', split_axis=2, concat_axis=0, tiled=True)  7.38 us
    all_to_all x2, local copies, waits for them, and re-layouts, shards(): lax.all_to_all(samples, 'panel', split_axis=2, concat_axis=0, tiled=True)  6.92 us
  transfers between devices with their start and end apart: 3, of which 3 were waited for; matrix products, arithmetic and copies ran while one was open for 1% of the time, Pallas kernels for 0%

commit v1 on v0

v1 whole, which is shorter than its diff:
```python
import math

import jax
import jax.numpy as jnp
from jax import lax
from jax.experimental import pallas as pl
from jax.experimental.pallas import tpu as pltpu
from jax.sharding import PartitionSpec as P

TIME = 1024
NF = 32
FBLK = 4


SPACING = 0.1


def make_table(time_rows, freq_bins):
    phase_index = freq_bins[None, :] * time_rows[:, None] % TIME
    angle_arg = 2.0 * math.pi / TIME * phase_index.astype(jnp.float32)
    window = 0.5 - 0.5 * jnp.cos(2.0 * math.pi / TIME * time_rows.astype(jnp.float32))
    weight = 2.0 / TIME * window[:, None]
    return jnp.concatenate(
        [weight * jnp.cos(angle_arg), -weight * jnp.sin(angle_arg)], axis=1
    ).astype(jnp.bfloat16)


def live_rows(counts):
    lane_ids = jnp.arange(128, dtype=jnp.int32)
    return (lane_ids[None, :] < counts[:, None]).astype(jnp.float32).reshape(-1)


def transform(window_table, turned):
    flat_samples = turned.reshape(window_table.shape[0], -1)
    raw_spectra = lax.dot_general(
        window_table, flat_samples, (((0,), (0,)), ((), ())), preferred_element_type=jnp.float32
    )
    return raw_spectra.reshape(2 * NF, 4, -1)


COS_FIT = (0.9999992221726555, -19.73898256405801, 64.92872767456161, -85.27240653862012, 58.794076313415644, -21.076836027706122)
SIN_FIT = (6.28305579836435, -41.33121428164835, 81.36681479714264, -74.47800123607628, 32.78139377750351)
CHUNK = 16
BLOCK = 128


def horner(fit, x):
    total = jnp.full_like(x, fit[-1])
    for c in fit[-2::-1]:
        total = total * x + c
    return total


def sum_four(x):
    return x + pltpu.roll(x, 1, 0) + pltpu.roll(x, 2, 0) + pltpu.roll(x, 3, 0)


def radiate_core(bins_ref, spec_ref, panel_ref, obs_ref, field_ref, turn_ref, green_ref, inv_ref, wave_ref):
    panels = panel_ref.shape[1]
    obs = obs_ref.shape[1]
    turned = panel_ref[...].T
    ox, oy, oz = obs_ref[0:1, :], obs_ref[1:2, :], obs_ref[2:3, :]
    for p in range(0, panels, CHUNK):
        rows = pl.ds(p, CHUNK)
        part = turned[p : p + CHUNK]
        dx, dy, dz = ox - part[:, 0:1], oy - part[:, 1:2], oz - part[:, 2:3]
        distance = jnp.sqrt(dx * dx + dy * dy + dz * dz)
        inverse = 1.0 / distance
        turn_ref[rows, :] = distance * (1.0 / (TIME * SPACING))
        green_ref[rows, :] = part[:, 3:4] * inverse * (1.0 / (4.0 * math.pi))
        inv_ref[rows, :] = inverse

    row = lax.broadcasted_iota(jnp.int32, (8, panels), 0)
    tail_row = lax.rem(row, 4) == 3
    sign = jnp.where(row < 4, -1.0, 1.0)
    place = jnp.where(tail_row, 0.0, jnp.where(row < 4, panel_ref[...], pltpu.roll(panel_ref[...], 4, 0)))
    live = panel_ref[4:5, :]
    obs_all = obs_ref[...]

    def one_bin(j, carry):
        bin_value = bins_ref[j].astype(jnp.float32)
        wavenumber = bin_value * (2.0 * math.pi / (TIME * SPACING))
        base = spec_ref[pl.ds(pl.multiple_of(j * 8, 8), 8), :] * live
        moment = sum_four(base * place)
        vec = jnp.where(tail_row, -moment, base)
        mono = jnp.where(tail_row, base, 0.0)
        vec_turn = sign * pltpu.roll(vec, 4, 0)
        mono_turn = sign * pltpu.roll(mono, 4, 0)
        coef = [wavenumber * mono_turn, wavenumber * mono, wavenumber * vec_turn, wavenumber * vec, vec, -vec_turn]
        total = jnp.zeros((16, obs), jnp.float32)
        for b in range(0, panels, BLOCK):
            for p in range(b, b + BLOCK, CHUNK):
                rows = pl.ds(p, CHUNK)
                turns = turn_ref[rows, :] * bin_value
                turns = turns - jnp.round(turns)
                square = turns * turns
                green = green_ref[rows, :]
                inverse = inv_ref[rows, :]
                real = horner(COS_FIT, square) * green
                imag = horner(SIN_FIT, square) * (turns * green)
                real1, imag1 = real * inverse, imag * inverse
                for s, w in enumerate((real, imag, real1, imag1, real1 * inverse, imag1 * inverse)):
                    wave_ref[pl.ds(b * 6 + s * BLOCK + p - b, CHUNK), :] = w.astype(jnp.bfloat16)
            left = jnp.concatenate([c[:, b : b + BLOCK] for c in coef], axis=1)
            high = left.astype(jnp.bfloat16)
            low = (left - high.astype(jnp.float32)).astype(jnp.bfloat16)
            total = total + jnp.dot(
                jnp.concatenate([high, low], axis=0),
                wave_ref[pl.ds(b * 6, 6 * BLOCK), :],
                preferred_element_type=jnp.float32,
            )
        both = sum_four((total[:8] + total[8:]) * obs_all)
        field_ref[pl.ds(j, 1), :] = both[3:4]
        field_ref[pl.ds(j + NF, 1), :] = both[7:8]
        return carry

    lax.fori_loop(0, NF, one_bin, 0)


def radiate(obs_position, panel_position, panel_area, live, spectra, freq_bins):
    panels = panel_area.shape[0]
    obs = obs_position.shape[1]
    order = spectra.reshape(2, NF, 4, panels).transpose(1, 0, 2, 3)
    order = jnp.concatenate([order[:, :, 1:], order[:, :, :1]], axis=2).reshape(NF * 8, panels)
    panel_rows = jnp.concatenate([panel_position, panel_area[None], live[None], jnp.zeros((3, panels), jnp.float32)])
    ones = jnp.ones((1, obs), jnp.float32)
    obs_rows = jnp.concatenate([obs_position, ones, obs_position, ones])
    vm = pl.BlockSpec(memory_space=pltpu.VMEM)
    return pl.pallas_call(
        radiate_core,
        out_shape=jax.ShapeDtypeStruct((2 * NF, obs), jnp.float32),
        in_specs=[pl.BlockSpec(memory_space=pltpu.SMEM), vm, vm, vm],
        out_specs=vm,
        scratch_shapes=[
            pltpu.VMEM((panels, obs), jnp.float32),
            pltpu.VMEM((panels, obs), jnp.float32),
            pltpu.VMEM((panels, obs), jnp.float32),
            pltpu.VMEM((panels * 6, obs), jnp.bfloat16),
        ],
        compiler_params=pltpu.CompilerParams(vmem_limit_bytes=32 * 1024 * 1024),
        name="radiate",
    )(freq_bins, order, panel_rows, obs_rows)


def shards(samples, panel_position, panel_area, panel_counts, obs_position, freq_bins):
    slab_len = samples.shape[0]
    panel_count = lax.axis_size("panel")
    obs_count = lax.axis_size("obs")
    source_slabs = jnp.arange(panel_count, dtype=jnp.int32)
    inner_step = jnp.arange(slab_len, dtype=jnp.int32)
    turned = lax.all_to_all(
        lax.all_to_all(samples, "panel", split_axis=2, concat_axis=0, tiled=True),
        "obs",
        split_axis=2,
        concat_axis=0,
        tiled=True,
    )
    quarters = jnp.arange(obs_count, dtype=jnp.int32)
    time_rows = (
        (source_slabs[None, :, None] * obs_count + quarters[:, None, None]) * slab_len
        + inner_step[None, None, :]
    ).reshape(-1)
    local_spectra = transform(make_table(time_rows, freq_bins), turned)
    spectra = lax.all_gather(local_spectra, "obs", axis=2, tiled=True)
    field = radiate(
        obs_position, panel_position, panel_area, live_rows(panel_counts), spectra, freq_bins
    )
    parts = field.T.reshape(panel_count, -1, 2 * NF)
    parts = lax.all_to_all(parts, "panel", split_axis=0, concat_axis=0, tiled=True)
    return jnp.sum(parts, axis=0).T.reshape(2, NF, -1)


def solution(mesh):
    in_specs = (
        P(("panel", "obs"), None, None),
        P(None, "panel"),
        P("panel"),
        P("panel"),
        P(None, "obs"),
        P(),
    )
    out_specs = P(None, None, ("obs", "panel"))
    return jax.shard_map(shards, mesh=mesh, in_specs=in_specs, out_specs=out_specs, check_vma=False)
```

time: 254 us -> 127 us (0.50)
  other arithmetic: 89.6 us -> 1.95 us
  waiting for transfers between devices: 96.5 us -> 39.1 us
  Pallas kernels: 0 us -> 26.5 us
  between operations: 13.6 us -> 0.17 us
  blocking collectives: 6.58 us -> 16.9 us
  local copies, waits for them, and re-layouts: 35.1 us -> 30.5 us
    reduce_sum x17 -> x1, other arithmetic: 84.5 us -> 0.02 us  [shards(): return jnp.sum(parts, axis=0).T.reshape(2, NF, -1)]
    unnamed x2 -> x0, waiting for transfers between devices: 59.7 us -> none
    pallas_call x0 -> x1, Pallas kernels: none -> 26.5 us  [radiate(): pl.pallas_call(radiate_core, out_shape=jax.ShapeDtypeStruct((2 * NF, obs)...]
    all_to_all x0 -> x1, blocking collectives: none -> 10.3 us  [shards(): lax.all_to_all(parts, 'panel', split_axis=0, concat_axis=0, tiled=True)]
    unnamed x18 -> x16, local copies, waits for them, and re-layouts: 23.2 us -> 20 us
  transfers between devices with their start and end apart: 3 -> 2, of which waited for: 3 -> 2; matrix products, arithmetic and copies ran while one was open for 1% -> 1% of each run, Pallas kernels for 0% -> 0%
where the time goes in v1:
time: 127 us; the launch traced here: 126 us
  waiting for transfers between devices  39.1 us (31%)
  local copies, waits for them, and re-layouts  30.5 us (24%)
  Pallas kernels  26.5 us (21%)
  blocking collectives  16.9 us (13%)
  starting transfers between devices  10.8 us (9%)
  other arithmetic  1.95 us (2%)
    pallas_call x1, Pallas kernels, radiate(): pl.pallas_call(radiate_core, out_shape=jax.ShapeDtypeStruct((2 * NF, obs)...  26.5 us
    all_to_all x1, waiting for transfers between devices, shards(): lax.all_to_all(samples, 'panel', split_axis=2, concat_axis=0, tiled=True)  25.4 us
    unnamed x16, local copies, waits for them, and re-layouts  20 us
    all_to_all x1, waiting for transfers between devices, shards(): lax.all_to_all(lax.all_to_all(samples, 'panel', split_axis=2, concat_axis...  13.6 us
    all_to_all x1, blocking collectives, shards(): lax.all_to_all(parts, 'panel', split_axis=0, concat_axis=0, tiled=True)  10.3 us
    all_to_all x1, starting transfers between devices, shards(): lax.all_to_all(samples, 'panel', split_axis=2, concat_axis=0, tiled=True)  7.25 us
    all_to_all x2, local copies, waits for them, and re-layouts, shards(): lax.all_to_all(samples, 'panel', split_axis=2, concat_axis=0, tiled=True)  6.98 us
    all_gather x1, blocking collectives, shards(): spectra = lax.all_gather(local_spectra, 'obs', axis=2, tiled=True)  6.58 us
  transfers between devices with their start and end apart: 2, of which 2 were waited for; matrix products, arithmetic and copies ran while one was open for 1% of the time, Pallas kernels for 0%

profile of v1, /device:TPU:0, one launch (start us, length us, event | category | flops | bytes accessed | tf_op | source)
XLA Modules:
  0.0 126.3 jit_solution(4149401223386758058)
XLA Ops:
  0.0 7.2 %copy.28 = bf16[32,4,4096]{0,1,2:T(4,128)(2,1)} copy(bf16[32,4,4096]{2,1,0:T(4,128)(2,1)} %param.6) | data formatting | bytes 2097152 | tf_op args[0]
  7.2 0.0 copy-start.4
  7.2 7.8 %reshape.122 = bf16[8,2,32768]{2,1,0:T(2,128)(2,1)} reshape(bf16[4096,4,32]{2,1,0:T(4,128)(2,1)} %bitcast.35) | data formatting | bytes 2097152
  15.1 7.3 %all-to-all-start = ((bf16[8,2,32768]{2,1,0:T(2,128)(2,1)}), bf16[8,2,32768]{2,1,0:T(2,128)(2,1)S(1)}, u32[]{:S(2)}, u32[]{:S(2)}) async-start(bf16[8,2,32768]{2,1,0:T(2,128)(2,1)} %reshape.122), calls=%async_computation | async-start | bytes 2097152 | tf_op jit(solution)/shard_map/all_to_all | solution.py:152
  22.3 0.1 iota_add_fusion
  22.4 0.1 add.85
  22.5 0.1 pad.7.clone
  22.6 0.0 copy-done.4
  22.6 0.1 fusion.6
  22.6 25.4 %all-to-all-done = bf16[8,2,32768]{2,1,0:T(2,128)(2,1)S(1)} async-done(((bf16[8,2,32768]{2,1,0:T(2,128)(2,1)}), bf16[8,2,32768]{2,1,0:T(2,128)(2,1)S(1)}, u32[]{:S(2)}, u32[]{:S(2)}) %all-to-all-start) | async-done | bytes 1048608 | tf_op jit(solution)/shard_map/all_to_all | solution.py:152
  48.1 4.5 %reshape.123 = bf16[4096,4,32]{2,1,0:T(4,128)(2,1)} reshape(bf16[8,2,32768]{2,1,0:T(2,128)(2,1)S(1)} %all-to-all-done) | data formatting | bytes 2097152
  52.6 0.0 copy-start.2
  52.6 0.0 copy-start.1
  52.6 0.0 copy-start.3
  52.6 0.0 copy-start
  52.6 5.6 %copy.39 = bf16[32,4,8,512]{3,0,2,1:T(8,128)(2,1)S(1)} copy(bf16[32,4,8,512]{0,1,3,2:T(4,128)(2,1)} %bitcast.34) | data formatting | bytes 2097152 | tf_op jit(solution)/shard_map/all_to_all | solution.py:152
  58.1 1.4 %copy.31 = bf16[256,4,512]{0,1,2:T(4,128)(2,1)} copy(bf16[256,4,512]{2,0,1:T(8,128)(2,1)S(1)} %bitcast.36) | data formatting | bytes 2097152 | tf_op jit(solution)/shard_map/all_to_all | solution.py:152
  59.6 3.5 %all-to-all-start.1 = ((bf16[256,4,512]{0,1,2:T(4,128)(2,1)}), bf16[256,4,512]{0,1,2:T(4,128)(2,1)S(1)}, u32[]{:S(2)}, u32[]{:S(2)}) async-start(bf16[256,4,512]{0,1,2:T(4,128)(2,1)} %copy.31), calls=%async_computation.1 | async-start | bytes 2097152 | tf_op jit(solution)/shard_map/all_to_all | solution.py:151
  63.1 0.0 copy-done.2
  63.2 0.0 copy-done.1
  63.2 0.0 copy-done.3
  63.2 0.1 maximum_maximum_fusion.panel_ref
  63.3 0.0 copy-done
  63.3 0.6 multiply_convert_fusion.1
  63.9 13.6 %all-to-all-done.1 = bf16[256,4,512]{0,1,2:T(4,128)(2,1)S(1)} async-done(((bf16[256,4,512]{0,1,2:T(4,128)(2,1)}), bf16[256,4,512]{0,1,2:T(4,128)(2,1)S(1)}, u32[]{:S(2)}, u32[]{:S(2)}) %all-to-all-start.1) | async-done | bytes 1048608 | tf_op jit(solution)/shard_map/all_to_all | solution.py:151
  77.5 0.1 copy.32
  77.7 0.7 copy.33
  78.3 0.2 copy.44
  78.5 0.5 copy.34
  79.1 0.4 fusion.3
  79.5 6.6 %all_gather.3 = f32[64,4,512]{2,0,1:T(8,128)S(1)} all-gather(f32[64,4,128]{2,0,1:T(8,128)S(1)} %fusion.3), channel_id=1, replica_groups=mesh['panel'=8,'obs'=4] {'obs'}, dimensions={2}, use_global_device_ids=true | all-gather | bytes 655360 | tf_op jit(solution)/shard_map/all_gather | solution.py:164
  86.1 0.3 copy.45
  86.4 0.1 slice.9
  86.5 0.1 slice.8
  86.7 0.3 pad_maximum_fusion
  86.9 0.2 reshape.117.spec_ref
  87.1 26.5 %radiate.1 = f32[64,256]{1,0:T(8,128)S(1)} custom-call(s32[32]{0:T(128)S(1)} %copy-done, f32[256,512]{1,0:T(8,128)S(1)} %reshape.117.spec_ref, f32[8,512]{1,0:T(8,128)S(1)} %maximum_maximum_fusion.panel_ref, f32[8,256]{1,0:T(8,128)S(1)} %pad_maximum_fusion.1.obs_ref), custom_call_target="tpu_custom_call" | custom-call | tf_op jit(solution)/shard_map/radiate/pallas_call | solution.py:129
  113.7 0.1 copy.36
  113.8 0.1 reshape.124
  113.9 10.3 %all_to_all.38 = f32[8,1,2048]{2,1,0:T(1,128)S(1)} all-to-all(f32[8,1,2048]{2,1,0:T(1,128)S(1)} %reshape.124), channel_id=1, replica_groups=mesh['panel'=8,'obs'=4] {'panel'}, dimensions={0} | all-to-all | bytes 131072 | tf_op jit(solution)/shard_map/all_to_all | solution.py:169
  124.2 0.5 broadcast.91
  124.7 0.8 reduce
  125.5 0.1 reshape.125
  125.6 0.7 copy.40
  (7 shorter events, 0.1 us)
Async XLA Ops:
  7.2 15.3 %copy-start.4 = (s32[4]{0:T(128)S(1)}, s32[4]{0:T(128)}, u32[]{:S(2)}) copy-start(s32[4]{0:T(128)} %param.9) | copy-start | bytes 52
  15.1 33.0 %all-to-all-start = ((bf16[8,2,32768]{2,1,0:T(2,128)(2,1)}), bf16[8,2,32768]{2,1,0:T(2,128)(2,1)S(1)}, u32[]{:S(2)}, u32[]{:S(2)}) async-start(bf16[8,2,32768]{2,1,0:T(2,128)(2,1)} %reshape.122), calls=%async_computation | async-start | bytes 2097152 | tf_op jit(solution)/shard_map/all_to_all | solution.py:152
  52.6 10.5 %copy-start.2 = (f32[3,256]{1,0:T(4,128)S(1)}, f32[3,256]{1,0:T(4,128)}, u32[]{:S(2)}) copy-start(f32[3,256]{1,0:T(4,128)} %param.10) | copy-start | bytes 9220
  52.6 10.6 %copy-start.1 = (f32[3,512]{1,0:T(4,128)S(1)}, f32[3,512]{1,0:T(4,128)}, u32[]{:S(2)}) copy-start(f32[3,512]{1,0:T(4,128)} %param.7) | copy-start | bytes 18436
  52.6 10.6 %copy-start.3 = (f32[512]{0:T(512)S(1)}, f32[512]{0:T(512)}, u32[]{:S(2)}) copy-start(f32[512]{0:T(512)} %param.8) | copy-start | bytes 6148
  52.6 10.7 %copy-start = (s32[32]{0:T(128)S(1)}, s32[32]{0:T(128)}, u32[]{:S(2)}) copy-start(s32[32]{0:T(128)} %bins_ref.1) | copy-start | bytes 388
  59.6 18.0 %all-to-all-start.1 = ((bf16[256,4,512]{0,1,2:T(4,128)(2,1)}), bf16[256,4,512]{0,1,2:T(4,128)(2,1)S(1)}, u32[]{:S(2)}, u32[]{:S(2)}) async-start(bf16[256,4,512]{0,1,2:T(4,128)(2,1)} %copy.31), calls=%async_computation.1 | async-start | bytes 2097152 | tf_op jit(solution)/shard_map/all_to_all | solution.py:151

commit v2 on v1

--- a/solution.py
+++ b/solution.py
@@ -1,3 +1,4 @@
+import functools
 import math
 
 import jax
@@ -13,16 +14,7 @@
 
 
 SPACING = 0.1
-
-
-def make_table(time_rows, freq_bins):
-    phase_index = freq_bins[None, :] * time_rows[:, None] % TIME
-    angle_arg = 2.0 * math.pi / TIME * phase_index.astype(jnp.float32)
-    window = 0.5 - 0.5 * jnp.cos(2.0 * math.pi / TIME * time_rows.astype(jnp.float32))
-    weight = 2.0 / TIME * window[:, None]
-    return jnp.concatenate(
-        [weight * jnp.cos(angle_arg), -weight * jnp.sin(angle_arg)], axis=1
-    ).astype(jnp.bfloat16)
+MESH = pl.DeviceIdType.MESH
 
 
 def live_rows(counts):
@@ -30,16 +22,9 @@
     return (lane_ids[None, :] < counts[:, None]).astype(jnp.float32).reshape(-1)
 
 
-def transform(window_table, turned):
-    flat_samples = turned.reshape(window_table.shape[0], -1)
-    raw_spectra = lax.dot_general(
-        window_table, flat_samples, (((0,), (0,)), ((), ())), preferred_element_type=jnp.float32
-    )
-    return raw_spectra.reshape(2 * NF, 4, -1)
-
-
 COS_FIT = (0.9999992221726555, -19.73898256405801, 64.92872767456161, -85.27240653862012, 58.794076313415644, -21.076836027706122)
 SIN_FIT = (6.28305579836435, -41.33121428164835, 81.36681479714264, -74.47800123607628, 32.78139377750351)
+SIN_FINE = (6.283182818550581, -41.34142139830231, 81.59618385833781, -76.5801003424203, 41.20539394682785, -12.271260758957148)
 CHUNK = 16
 BLOCK = 128
 
@@ -80,7 +65,8 @@
     def one_bin(j, carry):
         bin_value = bins_ref[j].astype(jnp.float32)
         wavenumber = bin_value * (2.0 * math.pi / (TIME * SPACING))
-        base = spec_ref[pl.ds(pl.multiple_of(j * 8, 8), 8), :] * live
+        rows_of_bin = pl.ds(pl.multiple_of(j * 8, 8), 8)
+        base = jnp.concatenate([spec_ref[q, rows_of_bin, :] for q in range(spec_ref.shape[0])], axis=1) * live
         moment = sum_four(base * place)
         vec = jnp.where(tail_row, -moment, base)
         mono = jnp.where(tail_row, base, 0.0)
@@ -120,8 +106,6 @@
 def radiate(obs_position, panel_position, panel_area, live, spectra, freq_bins):
     panels = panel_area.shape[0]
     obs = obs_position.shape[1]
-    order = spectra.reshape(2, NF, 4, panels).transpose(1, 0, 2, 3)
-    order = jnp.concatenate([order[:, :, 1:], order[:, :, :1]], axis=2).reshape(NF * 8, panels)
     panel_rows = jnp.concatenate([panel_position, panel_area[None], live[None], jnp.zeros((3, panels), jnp.float32)])
     ones = jnp.ones((1, obs), jnp.float32)
     obs_rows = jnp.concatenate([obs_position, ones, obs_position, ones])
@@ -139,29 +123,176 @@
         ],
         compiler_params=pltpu.CompilerParams(vmem_limit_bytes=32 * 1024 * 1024),
         name="radiate",
-    )(freq_bins, order, panel_rows, obs_rows)
+    )(freq_bins, spectra, panel_rows, obs_rows)
+
+
+def spectra_table(bin_rows, first_time, depth):
+    rows = bin_rows.shape[0]
+    row = lax.broadcasted_iota(jnp.int32, (rows, depth), 0)
+    column = lax.broadcasted_iota(jnp.int32, (rows, depth), 1)
+    time = first_time + (column >> 2)
+    index = (bin_rows * time) & (TIME - 1)
+    turns = index.astype(jnp.float32) * (1.0 / TIME)
+    turns = turns - jnp.round(turns)
+    real = horner(COS_FIT, turns * turns)
+    imag = -horner(SIN_FINE, turns * turns) * turns
+    window_turns = time.astype(jnp.float32) * (1.0 / TIME)
+    window_turns = window_turns - jnp.round(window_turns)
+    window = 0.5 - 0.5 * horner(COS_FIT, window_turns * window_turns)
+    weight = 2.0 / TIME * window
+    value = weight * jnp.where((row & 4) == 0, real, imag)
+    return jnp.where((row & 3) == ((column + 3) & 3), value, 0.0).astype(jnp.bfloat16)
+
+
+def spectra_kernel(
+    groups, width, samples_ref, bins_ref, out_ref, table, held, mine, send, arrived,
+    own_sem, sample_send, sample_recv, part_send, part_recv, sum_send, sum_recv,
+):
+    panel_count, obs_count = groups
+    panel, obs = lax.axis_index("panel"), lax.axis_index("obs")
+    slab = samples_ref.shape[0]
+    block = width * obs_count
+
+    barrier = pltpu.get_barrier_semaphore()
+    for k in range(1, obs_count):
+        pl.semaphore_signal(barrier, inc=1, device_id=(panel, lax.rem(obs + k, obs_count)), device_id_type=MESH)
+
+    def greet(k, carry):
+        pl.semaphore_signal(barrier, inc=1, device_id=(lax.rem(panel + k, panel_count), obs), device_id_type=MESH)
+        return carry
+
+    lax.fori_loop(1, panel_count, greet, 0)
+
+    def piece(step, part):
+        first = lax.rem(panel + 1 + step, panel_count) * block + part * width
+        return samples_ref.at[:, :, pl.ds(pl.multiple_of(first, 128), width)]
+
+    def own_copy(step):
+        return pltpu.make_async_copy(piece(step, obs), held.at[step, obs], own_sem.at[step])
+
+    def sample_copy(step, k):
+        other = lax.rem(obs + k, obs_count)
+        return pltpu.make_async_remote_copy(
+            src_ref=piece(step, other),
+            dst_ref=held.at[step, obs],
+            send_sem=sample_send.at[k - 1, step],
+            recv_sem=sample_recv.at[k - 1, step],
+            device_id=(panel, other),
+            device_id_type=MESH,
+        )
+
+    def part_copy(step):
+        return pltpu.make_async_remote_copy(
+            src_ref=send.at[step],
+            dst_ref=arrived.at[step],
+            send_sem=part_send.at[step],
+            recv_sem=part_recv.at[step],
+            device_id=(lax.rem(panel + 1 + step, panel_count), obs),
+            device_id_type=MESH,
+        )
+
+    def sum_copy(k):
+        return pltpu.make_async_remote_copy(
+            src_ref=out_ref.at[obs],
+            dst_ref=out_ref.at[obs],
+            send_sem=sum_send.at[k - 1],
+            recv_sem=sum_recv.at[k - 1],
+            device_id=(panel, lax.rem(obs + k, obs_count)),
+            device_id_type=MESH,
+        )
+
+    pl.semaphore_wait(barrier, obs_count + panel_count - 2)
+
+    def launch(step, carry):
+        for k in range(1, obs_count):
+            sample_copy(step, k).start()
+        own_copy(step).start()
+        return carry
+
+    lax.fori_loop(0, panel_count, launch, 0)
+    table[...] = spectra_table(bins_ref[...], panel * obs_count * slab, table.shape[1])
+
+    def transform(step):
+        own_copy(step).wait()
+        for k in range(1, obs_count):
+            sample_copy(step, k).wait_recv()
+        return jnp.dot(
+            table[...], held[step].reshape(table.shape[1], width), preferred_element_type=jnp.float32
+        )
+
+    def one_step(step, carry):
+        send[step] = transform(step).astype(jnp.bfloat16)
+        part_copy(step).start()
+        return carry
+
+    lax.fori_loop(0, panel_count - 1, one_step, 0)
+    mine[...] = transform(panel_count - 1)
+
+    def add(step, carry):
+        part_copy(step).wait_recv()
+        mine[...] += arrived[step].astype(jnp.float32)
+        return carry
+
+    lax.fori_loop(0, panel_count - 1, add, 0)
+    out_ref[obs] = mine[...]
+    for k in range(1, obs_count):
+        sum_copy(k).start()
+    for k in range(1, obs_count):
+        sum_copy(k).wait_recv()
+
+    def drain(step, carry):
+        for k in range(1, obs_count):
+            sample_copy(step, k).wait_send()
+        return carry
+
+    lax.fori_loop(0, panel_count, drain, 0)
+
+    def drain_parts(step, carry):
+        part_copy(step).wait_send()
+        return carry
+
+    lax.fori_loop(0, panel_count - 1, drain_parts, 0)
+    for k in range(1, obs_count):
+        sum_copy(k).wait_send()
+
+
+def all_spectra(samples, freq_bins, panel_count, obs_count):
+    slab, channels, panels = samples.shape
+    width = panels // (panel_count * obs_count)
+    rows = 2 * NF * channels
+    depth = slab * channels * obs_count
+    bin_rows = jnp.repeat(freq_bins, 2 * channels)[:, None]
+    dma = pltpu.SemaphoreType.DMA
+    return pl.pallas_call(
+        functools.partial(spectra_kernel, (panel_count, obs_count), width),
+        out_shape=jax.ShapeDtypeStruct((obs_count, rows, width), jnp.float32),
+        in_specs=[pl.BlockSpec(memory_space=pl.ANY), pl.BlockSpec(memory_space=pltpu.VMEM)],
+        out_specs=pl.BlockSpec(memory_space=pltpu.VMEM),
+        scratch_shapes=[
+            pltpu.VMEM((rows, depth), jnp.bfloat16),
+            pltpu.VMEM((panel_count, obs_count, slab, channels, width), jnp.bfloat16),
+            pltpu.VMEM((rows, width), jnp.float32),
+            pltpu.VMEM((panel_count - 1, rows, width), jnp.bfloat16),
+            pltpu.VMEM((panel_count - 1, rows, width), jnp.bfloat16),
+            dma((panel_count,)),
+            dma((obs_count - 1, panel_count)),
+            dma((obs_count - 1, panel_count)),
+            dma((panel_count - 1,)),
+            dma((panel_count - 1,)),
+            dma((obs_count - 1,)),
+            dma((obs_count - 1,)),
+        ],
+        compiler_params=pltpu.CompilerParams(
+            collective_id=0, has_side_effects=True, vmem_limit_bytes=40 * 1024 * 1024
+        ),
+        name="spectra",
+    )(samples, bin_rows)
 
 
 def shards(samples, panel_position, panel_area, panel_counts, obs_position, freq_bins):
-    slab_len = samples.shape[0]
     panel_count = lax.axis_size("panel")
     obs_count = lax.axis_size("obs")
-    source_slabs = jnp.arange(panel_count, dtype=jnp.int32)
-    inner_step = jnp.arange(slab_len, dtype=jnp.int32)
-    turned = lax.all_to_all(
-        lax.all_to_all(samples, "panel", split_axis=2, concat_axis=0, tiled=True),
-        "obs",
-        split_axis=2,
-        concat_axis=0,
-        tiled=True,
-    )
-    quarters = jnp.arange(obs_count, dtype=jnp.int32)
-    time_rows = (
-        (source_slabs[None, :, None] * obs_count + quarters[:, None, None]) * slab_len
-        + inner_step[None, None, :]
-    ).reshape(-1)
-    local_spectra = transform(make_table(time_rows, freq_bins), turned)
-    spectra = lax.all_gather(local_spectra, "obs", axis=2, tiled=True)
+    spectra = all_spectra(samples, freq_bins, panel_count, obs_count)
     field = radiate(
         obs_position, panel_position, panel_area, live_rows(panel_counts), spectra, freq_bins
     )

time: 127 us -> 76.8 us (0.60)
  waiting for transfers between devices: 39.1 us -> 0 us
  Pallas kernels: 26.5 us -> 56.5 us
  local copies, waits for them, and re-layouts: 30.5 us -> 6.05 us
  starting transfers between devices: 10.8 us -> 0 us
  blocking collectives: 16.9 us -> 12.9 us
    all_to_all x2 -> x0, waiting for transfers between devices: 39.1 us -> none  [the longest x1 25.4 us: shards(): lax.all_to_all(samples, 'panel', split_axis=2, concat_axis=0, tiled=True)]
    pallas_call x0 -> x1, Pallas kernels: none -> 29.9 us  [all_spectra(): pl.pallas_call(functools.partial(spectra_kernel, (panel_count, obs_count)...]
    unnamed x16 -> x14, local copies, waits for them, and re-layouts: 20 us -> 3.85 us
    all_to_all x2 -> x0, starting transfers between devices: 10.8 us -> none  [the longest x1 7.25 us: shards(): lax.all_to_all(samples, 'panel', split_axis=2, concat_axis=0, tiled=True)]
    all_to_all x4 -> x0, local copies, waits for them, and re-layouts: 7.78 us -> none  [the longest x2 6.98 us: shards(): lax.all_to_all(samples, 'panel', split_axis=2, concat_axis=0, tiled=True)]
    all_gather x1 -> x0, blocking collectives: 6.58 us -> none  [shards(): spectra = lax.all_gather(local_spectra, 'obs', axis=2, tiled=True)]
    all_to_all x1, blocking collectives: 10.3 us -> 12.9 us  [shards(): lax.all_to_all(parts, 'panel', split_axis=0, concat_axis=0, tiled=True)]
  transfers between devices with their start and end apart: 2 -> 0, of which waited for: 2 -> 0; matrix products, arithmetic and copies ran while one was open for 1% -> 0% of each run, Pallas kernels for 0% -> 0%
where the time goes in v2:
time: 76.8 us; the launch traced here: 76.5 us
  Pallas kernels  56.5 us (74%)
  blocking collectives  12.9 us (17%)
  local copies, waits for them, and re-layouts  6.05 us (8%)
  other arithmetic  0.97 us (1%)
    pallas_call x1, Pallas kernels, all_spectra(): pl.pallas_call(functools.partial(spectra_kernel, (panel_count, obs_count)...  29.9 us
    pallas_call x1, Pallas kernels, radiate(): pl.pallas_call(radiate_core, out_shape=jax.ShapeDtypeStruct((2 * NF, obs)...  26.6 us
    all_to_all x1, blocking collectives, shards(): lax.all_to_all(parts, 'panel', split_axis=0, concat_axis=0, tiled=True)  12.9 us
    unnamed x14, local copies, waits for them, and re-layouts  3.85 us

profile of v2, /device:TPU:0, one launch (start us, length us, event | category | flops | bytes accessed | tf_op | source)
XLA Modules:
  0.0 76.5 jit_solution(13147717259509142631)
XLA Ops:
  0.0 0.7 broadcast_in_dim.14
  0.7 0.0 copy-start.5
  0.7 0.1 broadcast_in_dim_reshape.5.bins_ref
  0.8 0.6 copy-done.5
  1.4 0.1 fusion
  1.5 0.0 copy-start
  1.5 1.2 %copy-done = bf16[32,4,4096]{2,1,0:T(4,128)(2,1)S(1)} copy-done((bf16[32,4,4096]{2,1,0:T(4,128)(2,1)S(1)}, bf16[32,4,4096]{2,1,0:T(4,128)(2,1)}, u32[]{:S(2)}) %copy-start) | copy-done | bytes 1048600
  2.7 29.9 %spectra.1.spec_ref = f32[4,256,128]{2,1,0:T(8,128)S(1)} custom-call(bf16[32,4,4096]{2,1,0:T(4,128)(2,1)S(1)} %copy-done, s32[256,1]{1,0:T(8,128)S(1)} %broadcast_in_dim_reshape.5.bins_ref), custom_call_target="tpu_custom_call" | custom-call | tf_op jit(solution)/shard_map/spectra/pallas_call | solution.py:266
  32.6 0.0 copy-start.3
  32.6 0.1 pad.7.clone
  32.7 0.6 copy-done.3
  33.3 0.0 copy-start.2
  33.3 0.0 copy-start.4
  33.3 0.7 copy-done.2
  34.0 0.0 copy-done.4
  34.0 0.0 copy-start.1
  34.0 0.1 maximum_maximum_fusion.panel_ref
  34.1 0.6 copy-done.1
  34.7 26.6 %radiate.1 = f32[64,256]{1,0:T(8,128)S(1)} custom-call(s32[32]{0:T(128)S(1)} %copy-done.1, f32[4,256,128]{2,1,0:T(8,128)S(1)} %spectra.1.spec_ref, f32[8,512]{1,0:T(8,128)S(1)} %maximum_maximum_fusion.panel_ref, f32[8,256]{1,0:T(8,128)S(1)} %pad_maximum_fusion.obs_ref), custom_call_target="tpu_custom_call" | custom-call | tf_op jit(solution)/shard_map/radiate/pallas_call | solution.py:113
  61.2 0.1 copy.10
  61.3 0.1 reshape.37
  61.5 12.9 %all_to_all.5 = f32[8,1,2048]{2,1,0:T(1,128)S(1)} all-to-all(f32[8,1,2048]{2,1,0:T(1,128)S(1)} %reshape.37), channel_id=1, replica_groups=mesh['panel'=8,'obs'=4] {'panel'}, dimensions={0} | all-to-all | bytes 131072 | tf_op jit(solution)/shard_map/all_to_all | solution.py:300
  74.4 0.5 broadcast.7
  74.9 0.8 %reduce = f32[8,2048]{1,0:T(8,128)S(1)} reduce(f32[8,1,2048]{2,1,0:T(1,128)S(1)} %all_to_all.5, f32[]{:T(128)} %broadcast.7), dimensions={1}, to_apply=%all_to_all.3.reduce_sub_computation | reduce | bytes 131076 | tf_op jit(solution)/shard_map/all_to_all | solution.py:300
  75.7 0.1 reshape.38
  75.8 0.7 copy.12
  (4 shorter events, 0.0 us)
Async XLA Ops:
  0.7 0.7 copy-start.5
  1.5 1.2 %copy-start = (bf16[32,4,4096]{2,1,0:T(4,128)(2,1)S(1)}, bf16[32,4,4096]{2,1,0:T(4,128)(2,1)}, u32[]{:S(2)}) copy-start(bf16[32,4,4096]{2,1,0:T(4,128)(2,1)} %samples_ref.1) | copy-start | bytes 3145732
  32.6 0.7 copy-start.3
  33.3 0.7 copy-start.2
  33.3 0.7 copy-start.4
  34.0 0.7 copy-start.1

commit v3 on v2

--- a/solution.py
+++ b/solution.py
@@ -126,12 +126,11 @@
     )(freq_bins, spectra, panel_rows, obs_rows)
 
 
-def spectra_table(bin_rows, first_time, depth):
-    rows = bin_rows.shape[0]
-    row = lax.broadcasted_iota(jnp.int32, (rows, depth), 0)
-    column = lax.broadcasted_iota(jnp.int32, (rows, depth), 1)
+def spectra_table(first_bin, second_bin, first_time, depth):
+    row = lax.broadcasted_iota(jnp.int32, (16, depth), 0)
+    column = lax.broadcasted_iota(jnp.int32, (16, depth), 1)
     time = first_time + (column >> 2)
-    index = (bin_rows * time) & (TIME - 1)
+    index = (jnp.where(row < 8, first_bin, second_bin) * time) & (TIME - 1)
     turns = index.astype(jnp.float32) * (1.0 / TIME)
     turns = turns - jnp.round(turns)
     real = horner(COS_FIT, turns * turns)
@@ -210,7 +209,15 @@
         return carry
 
     lax.fori_loop(0, panel_count, launch, 0)
-    table[...] = spectra_table(bins_ref[...], panel * obs_count * slab, table.shape[1])
+    first_time = panel * obs_count * slab
+
+    def two_bins(i, carry):
+        table[pl.ds(pl.multiple_of(i * 16, 16), 16), :] = spectra_table(
+            bins_ref[2 * i], bins_ref[2 * i + 1], first_time, table.shape[1]
+        )
+        return carry
+
+    lax.fori_loop(0, NF // 2, two_bins, 0)
 
     def transform(step):
         own_copy(step).wait()
@@ -261,12 +268,11 @@
     width = panels // (panel_count * obs_count)
     rows = 2 * NF * channels
     depth = slab * channels * obs_count
-    bin_rows = jnp.repeat(freq_bins, 2 * channels)[:, None]
     dma = pltpu.SemaphoreType.DMA
     return pl.pallas_call(
         functools.partial(spectra_kernel, (panel_count, obs_count), width),
         out_shape=jax.ShapeDtypeStruct((obs_count, rows, width), jnp.float32),
-        in_specs=[pl.BlockSpec(memory_space=pl.ANY), pl.BlockSpec(memory_space=pltpu.VMEM)],
+        in_specs=[pl.BlockSpec(memory_space=pl.ANY), pl.BlockSpec(memory_space=pltpu.SMEM)],
         out_specs=pl.BlockSpec(memory_space=pltpu.VMEM),
         scratch_shapes=[
             pltpu.VMEM((rows, depth), jnp.bfloat16),
@@ -286,7 +292,78 @@
             collective_id=0, has_side_effects=True, vmem_limit_bytes=40 * 1024 * 1024
         ),
         name="spectra",
-    )(samples, bin_rows)
+    )(samples, freq_bins)
+
+
+def collect_kernel(panel_count, field_ref, out_ref, staged, arrived, send_sem, recv_sem):
+    panel, obs = lax.axis_index("panel"), lax.axis_index("obs")
+    rows = staged.shape[1]
+
+    barrier = pltpu.get_barrier_semaphore()
+
+    def greet(k, carry):
+        pl.semaphore_signal(barrier, inc=1, device_id=(lax.rem(panel + k, panel_count), obs), device_id_type=MESH)
+        return carry
+
+    lax.fori_loop(1, panel_count, greet, 0)
+    field = field_ref[...]
+    turned = jnp.concatenate([field, jnp.zeros((128 - field.shape[0], field.shape[1]), jnp.float32)], axis=0).T
+    for b in range(panel_count):
+        staged[b] = turned[b * rows : (b + 1) * rows]
+
+    def copy(k):
+        other = lax.rem(panel + k, panel_count)
+        return pltpu.make_async_remote_copy(
+            src_ref=staged.at[other],
+            dst_ref=arrived.at[k - 1],
+            send_sem=send_sem.at[k - 1],
+            recv_sem=recv_sem.at[k - 1],
+            device_id=(other, obs),
+            device_id_type=MESH,
+        )
+
+    pl.semaphore_wait(barrier, panel_count - 1)
+
+    def launch(k, carry):
+        copy(k).start()
+        return carry
+
+    lax.fori_loop(1, panel_count, launch, 0)
+
+    def add(k, total):
+        copy(k).wait_recv()
+        return total + arrived[k - 1]
+
+    total = lax.fori_loop(1, panel_count, add, staged[panel])
+    out_ref[...] = total
+
+    def drain(k, carry):
+        copy(k).wait_send()
+        return carry
+
+    lax.fori_loop(1, panel_count, drain, 0)
+
+
+def collect(field, panel_count):
+    rows = field.shape[1] // panel_count
+    dma = pltpu.SemaphoreType.DMA
+    vm = pl.BlockSpec(memory_space=pltpu.VMEM)
+    return pl.pallas_call(
+        functools.partial(collect_kernel, panel_count),
+        out_shape=jax.ShapeDtypeStruct((rows, 128), jnp.float32),
+        in_specs=[vm],
+        out_specs=vm,
+        scratch_shapes=[
+            pltpu.VMEM((panel_count, rows, 128), jnp.float32),
+            pltpu.VMEM((panel_count - 1, rows, 128), jnp.float32),
+            dma((panel_count - 1,)),
+            dma((panel_count - 1,)),
+        ],
+        compiler_params=pltpu.CompilerParams(
+            collective_id=1, has_side_effects=True, vmem_limit_bytes=16 * 1024 * 1024
+        ),
+        name="collect",
+    )(field)
 
 
 def shards(samples, panel_position, panel_area, panel_counts, obs_position, freq_bins):
@@ -296,9 +373,8 @@
     field = radiate(
         obs_position, panel_position, panel_area, live_rows(panel_counts), spectra, freq_bins
     )
-    parts = field.T.reshape(panel_count, -1, 2 * NF)
-    parts = lax.all_to_all(parts, "panel", split_axis=0, concat_axis=0, tiled=True)
-    return jnp.sum(parts, axis=0).T.reshape(2, NF, -1)
+    total = collect(field, panel_count)[:, : 2 * NF]
+    return total.T.reshape(2, NF, -1)
 
 
 def solution(mesh):

time: 76.8 us -> 70.3 us (0.915)
  blocking collectives: 12.9 us -> 0 us
  Pallas kernels: 56.5 us -> 66 us
  local copies, waits for them, and re-layouts: 6.05 us -> 3.84 us
  other arithmetic: 0.97 us -> 0.15 us
    all_to_all x1 -> x0, blocking collectives: 12.9 us -> none  [shards(): lax.all_to_all(parts, 'panel', split_axis=0, concat_axis=0, tiled=True)]
    pallas_call x0 -> x1, Pallas kernels: none -> 8.87 us  [collect(): pl.pallas_call(functools.partial(collect_kernel, panel_count), out_shape=...]
    all_to_all x1 -> x0, other arithmetic: 0.8 us -> none  [shards(): lax.all_to_all(parts, 'panel', split_axis=0, concat_axis=0, tiled=True)]
    unnamed x14 -> x12, local copies, waits for them, and re-layouts: 3.85 us -> 3.06 us
where the time goes in v3:
time: 70.3 us; the launch traced here: 70 us
  Pallas kernels  66 us (94%)
  local copies, waits for them, and re-layouts  3.84 us (5%)
    pallas_call x1, Pallas kernels, all_spectra(): pl.pallas_call(functools.partial(spectra_kernel, (panel_count, obs_count)...  30.6 us
    pallas_call x1, Pallas kernels, radiate(): pl.pallas_call(radiate_core, out_shape=jax.ShapeDtypeStruct((2 * NF, obs)...  26.6 us
    pallas_call x1, Pallas kernels, collect(): pl.pallas_call(functools.partial(collect_kernel, panel_count), out_shape=...  8.87 us
    unnamed x12, local copies, waits for them, and re-layouts  3.06 us

profile of v3, /device:TPU:0, one launch (start us, length us, event | category | flops | bytes accessed | tf_op | source)
XLA Modules:
  0.0 70.0 jit_solution(4462095048963514413)
XLA Ops:
  0.0 0.0 copy-start.5
  0.0 0.0 copy-start.3
  0.0 0.1 pad.7.clone
  0.1 0.6 copy-done.5
  0.7 0.1 fusion
  0.7 0.0 copy-start.2
  0.7 0.0 copy-done.3
  0.7 0.0 copy-start.4
  0.8 0.7 copy-done.2
  1.4 0.0 copy-done.4
  1.4 0.0 copy-start.1
  1.4 0.1 maximum_maximum_fusion.panel_ref
  1.5 0.6 copy-done.1
  2.1 0.0 copy-start
  2.1 1.2 %copy-done = bf16[32,4,4096]{2,1,0:T(4,128)(2,1)S(1)} copy-done((bf16[32,4,4096]{2,1,0:T(4,128)(2,1)S(1)}, bf16[32,4,4096]{2,1,0:T(4,128)(2,1)}, u32[]{:S(2)}) %copy-start) | copy-done | bytes 1048600
  3.3 30.6 %spectra.1.spec_ref = f32[4,256,128]{2,1,0:T(8,128)S(1)} custom-call(bf16[32,4,4096]{2,1,0:T(4,128)(2,1)S(1)} %copy-done, s32[32]{0:T(128)S(1)} %copy-done.1), custom_call_target="tpu_custom_call" | custom-call | tf_op jit(solution)/shard_map/spectra/pallas_call | solution.py:272
  33.9 26.6 %radiate.1.field_ref = f32[64,256]{1,0:T(8,128)S(1)} custom-call(s32[32]{0:T(128)S(1)} %copy-done.1, f32[4,256,128]{2,1,0:T(8,128)S(1)} %spectra.1.spec_ref, f32[8,512]{1,0:T(8,128)S(1)} %maximum_maximum_fusion.panel_ref, f32[8,256]{1,0:T(8,128)S(1)} %pad_maximum_fusion.obs_ref), custom_call_target="tpu_custom_call" | custom-call | tf_op jit(solution)/shard_map/radiate/pallas_call | solution.py:113
  60.4 8.9 %collect.1 = f32[32,128]{1,0:T(8,128)S(1)} custom-call(f32[64,256]{1,0:T(8,128)S(1)} %radiate.1.field_ref), custom_call_target="tpu_custom_call" | custom-call | tf_op jit(solution)/shard_map/collect/pallas_call | solution.py:351
  69.3 0.7 copy.8
  (4 shorter events, 0.0 us)
Async XLA Ops:
  0.0 0.7 copy-start.5
  0.0 0.7 %copy-start.3 = (f32[3,256]{1,0:T(4,128)S(1)}, f32[3,256]{1,0:T(4,128)}, u32[]{:S(2)}) copy-start(f32[3,256]{1,0:T(4,128)} %param.10) | copy-start | bytes 9220
  0.7 0.7 copy-start.2
  0.7 0.7 copy-start.4
  1.4 0.7 copy-start.1
  2.1 1.2 %copy-start = (bf16[32,4,4096]{2,1,0:T(4,128)(2,1)S(1)}, bf16[32,4,4096]{2,1,0:T(4,128)(2,1)}, u32[]{:S(2)}) copy-start(bf16[32,4,4096]{2,1,0:T(4,128)(2,1)} %samples_ref.1) | copy-start | bytes 3145732

commit v4 on v3

--- a/solution.py
+++ b/solution.py
@@ -40,7 +40,7 @@
     return x + pltpu.roll(x, 1, 0) + pltpu.roll(x, 2, 0) + pltpu.roll(x, 3, 0)
 
 
-def radiate_core(bins_ref, spec_ref, panel_ref, obs_ref, field_ref, turn_ref, green_ref, inv_ref, wave_ref):
+def radiate_core(bins_ref, spec_ref, panel_ref, obs_ref, field_ref, turn_ref, green_ref, inv_ref, short_ref, wave_ref):
     panels = panel_ref.shape[1]
     obs = obs_ref.shape[1]
     turned = panel_ref[...].T
@@ -54,6 +54,7 @@
         turn_ref[rows, :] = distance * (1.0 / (TIME * SPACING))
         green_ref[rows, :] = part[:, 3:4] * inverse * (1.0 / (4.0 * math.pi))
         inv_ref[rows, :] = inverse
+        short_ref[rows, :] = inverse.astype(jnp.bfloat16)
 
     row = lax.broadcasted_iota(jnp.int32, (8, panels), 0)
     tail_row = lax.rem(row, 4) == 3
@@ -62,7 +63,7 @@
     live = panel_ref[4:5, :]
     obs_all = obs_ref[...]
 
-    def one_bin(j, carry):
+    def one_bin(j, slot):
         bin_value = bins_ref[j].astype(jnp.float32)
         wavenumber = bin_value * (2.0 * math.pi / (TIME * SPACING))
         rows_of_bin = pl.ds(pl.multiple_of(j * 8, 8), 8)
@@ -85,22 +86,29 @@
                 real = horner(COS_FIT, square) * green
                 imag = horner(SIN_FIT, square) * (turns * green)
                 real1, imag1 = real * inverse, imag * inverse
-                for s, w in enumerate((real, imag, real1, imag1, real1 * inverse, imag1 * inverse)):
-                    wave_ref[pl.ds(b * 6 + s * BLOCK + p - b, CHUNK), :] = w.astype(jnp.bfloat16)
+                waves = [w.astype(jnp.bfloat16) for w in (real, imag, real1, imag1)]
+                short = short_ref[rows, :]
+                waves += [waves[2] * short, waves[3] * short]
+                for s, w in enumerate(waves):
+                    wave_ref[slot, pl.ds(b * 6 + s * BLOCK + p - b, CHUNK), :] = w
             left = jnp.concatenate([c[:, b : b + BLOCK] for c in coef], axis=1)
             high = left.astype(jnp.bfloat16)
             low = (left - high.astype(jnp.float32)).astype(jnp.bfloat16)
             total = total + jnp.dot(
                 jnp.concatenate([high, low], axis=0),
-                wave_ref[pl.ds(b * 6, 6 * BLOCK), :],
+                wave_ref[slot, pl.ds(b * 6, 6 * BLOCK), :],
                 preferred_element_type=jnp.float32,
             )
         both = sum_four((total[:8] + total[8:]) * obs_all)
         field_ref[pl.ds(j, 1), :] = both[3:4]
         field_ref[pl.ds(j + NF, 1), :] = both[7:8]
-        return carry
-
-    lax.fori_loop(0, NF, one_bin, 0)
+
+    def two_bins(i, carry):
+        one_bin(2 * i, 0)
+        one_bin(2 * i + 1, 1)
+        return carry
+
+    lax.fori_loop(0, NF // 2, two_bins, 0)
 
 
 def radiate(obs_position, panel_position, panel_area, live, spectra, freq_bins):
@@ -119,7 +127,8 @@
             pltpu.VMEM((panels, obs), jnp.float32),
             pltpu.VMEM((panels, obs), jnp.float32),
             pltpu.VMEM((panels, obs), jnp.float32),
-            pltpu.VMEM((panels * 6, obs), jnp.bfloat16),
+            pltpu.VMEM((panels, obs), jnp.bfloat16),
+            pltpu.VMEM((2, panels * 6, obs), jnp.bfloat16),
         ],
         compiler_params=pltpu.CompilerParams(vmem_limit_bytes=32 * 1024 * 1024),
         name="radiate",

time: 70.3 us -> 65.4 us (0.930)
  Pallas kernels: 66 us -> 61.1 us
    pallas_call x1, Pallas kernels: 26.6 us -> 21.7 us  [radiate(): pl.pallas_call(radiate_core, out_shape=jax.ShapeDtypeStruct((2 * NF, obs)...]
where the time goes in v4:
time: 65.4 us; the launch traced here: 65.2 us
  Pallas kernels  61.1 us (93%)
  local copies, waits for them, and re-layouts  3.84 us (6%)
    pallas_call x1, Pallas kernels, all_spectra(): pl.pallas_call(functools.partial(spectra_kernel, (panel_count, obs_count)...  30.6 us
    pallas_call x1, Pallas kernels, radiate(): pl.pallas_call(radiate_core, out_shape=jax.ShapeDtypeStruct((2 * NF, obs)...  21.7 us
    pallas_call x1, Pallas kernels, collect(): pl.pallas_call(functools.partial(collect_kernel, panel_count), out_shape=...  8.87 us
    unnamed x12, local copies, waits for them, and re-layouts  3.06 us

profile of v4, /device:TPU:0, one launch (start us, length us, event | category | flops | bytes accessed | tf_op | source)
XLA Modules:
  0.0 65.2 jit_solution(9564536647134734946)
XLA Ops:
  0.0 0.0 copy-start.5
  0.0 0.0 copy-start.3
  0.0 0.1 pad.7.clone
  0.1 0.6 copy-done.5
  0.7 0.1 fusion
  0.7 0.0 copy-start.2
  0.7 0.0 copy-done.3
  0.7 0.0 copy-start.4
  0.8 0.7 %copy-done.2 = f32[3,512]{1,0:T(4,128)S(1)} copy-done((f32[3,512]{1,0:T(4,128)S(1)}, f32[3,512]{1,0:T(4,128)}, u32[]{:S(2)}) %copy-start.2) | copy-done | bytes 6168
  1.4 0.0 copy-done.4
  1.4 0.0 copy-start.1
  1.4 0.1 maximum_maximum_fusion.panel_ref
  1.5 0.6 copy-done.1
  2.1 0.0 copy-start
  2.1 1.2 %copy-done = bf16[32,4,4096]{2,1,0:T(4,128)(2,1)S(1)} copy-done((bf16[32,4,4096]{2,1,0:T(4,128)(2,1)S(1)}, bf16[32,4,4096]{2,1,0:T(4,128)(2,1)}, u32[]{:S(2)}) %copy-start) | copy-done | bytes 1048600
  3.3 30.6 %spectra.1.spec_ref = f32[4,256,128]{2,1,0:T(8,128)S(1)} custom-call(bf16[32,4,4096]{2,1,0:T(4,128)(2,1)S(1)} %copy-done, s32[32]{0:T(128)S(1)} %copy-done.1), custom_call_target="tpu_custom_call" | custom-call | tf_op jit(solution)/shard_map/spectra/pallas_call | solution.py:281
  33.9 21.7 %radiate.1.field_ref = f32[64,256]{1,0:T(8,128)S(1)} custom-call(s32[32]{0:T(128)S(1)} %copy-done.1, f32[4,256,128]{2,1,0:T(8,128)S(1)} %spectra.1.spec_ref, f32[8,512]{1,0:T(8,128)S(1)} %maximum_maximum_fusion.panel_ref, f32[8,256]{1,0:T(8,128)S(1)} %pad_maximum_fusion.obs_ref), custom_call_target="tpu_custom_call" | custom-call | tf_op jit(solution)/shard_map/radiate/pallas_call | solution.py:121
  55.6 8.9 %collect.1 = f32[32,128]{1,0:T(8,128)S(1)} custom-call(f32[64,256]{1,0:T(8,128)S(1)} %radiate.1.field_ref), custom_call_target="tpu_custom_call" | custom-call | tf_op jit(solution)/shard_map/collect/pallas_call | solution.py:360
  64.5 0.7 %copy.8 = f32[64,32]{1,0:T(8,128)} copy(f32[64,32]{0,1:T(8,128)S(1)} %slice_bitcast_fusion) | data formatting | bytes 16384 | tf_op jit(solution)/shard_map/reshape | solution.py:386
  (4 shorter events, 0.0 us)
Async XLA Ops:
  0.0 0.7 %copy-start.5 = (s32[4]{0:T(128)S(1)}, s32[4]{0:T(128)}, u32[]{:S(2)}) copy-start(s32[4]{0:T(128)} %param.9) | copy-start | bytes 52
  0.0 0.7 %copy-start.3 = (f32[3,256]{1,0:T(4,128)S(1)}, f32[3,256]{1,0:T(4,128)}, u32[]{:S(2)}) copy-start(f32[3,256]{1,0:T(4,128)} %param.10) | copy-start | bytes 9220
  0.7 0.7 %copy-start.2 = (f32[3,512]{1,0:T(4,128)S(1)}, f32[3,512]{1,0:T(4,128)}, u32[]{:S(2)}) copy-start(f32[3,512]{1,0:T(4,128)} %param.7) | copy-start | bytes 18436
  0.7 0.7 %copy-start.4 = (f32[512]{0:T(512)S(1)}, f32[512]{0:T(512)}, u32[]{:S(2)}) copy-start(f32[512]{0:T(512)} %param.8) | copy-start | bytes 6148
  1.4 0.7 %copy-start.1 = (s32[32]{0:T(128)S(1)}, s32[32]{0:T(128)}, u32[]{:S(2)}) copy-start(s32[32]{0:T(128)} %bins_ref.3) | copy-start | bytes 388
  2.1 1.2 %copy-start = (bf16[32,4,4096]{2,1,0:T(4,128)(2,1)S(1)}, bf16[32,4,4096]{2,1,0:T(4,128)(2,1)}, u32[]{:S(2)}) copy-start(bf16[32,4,4096]{2,1,0:T(4,128)(2,1)} %samples_ref.1) | copy-start | bytes 3145732
